TPU v7x, 512 devices: a whole 4x8x8 slice. The times are simulated.
512 devices in a mesh: grp: 16 (over y, x_hi), blk: 32 (over x_lo, z, core).
Axes of the slice: x: 4 (x_hi: 2, x_lo: 2; x = x_hi * 2 + x_lo), y: 8, z: 8, core: 2. Of those that a mesh axis runs over, the one named last changes fastest.
Arguments:
- images: bfloat16 [65536, 1152], P(('grp', 'blk')), may hold values from -6 to 6
- texts: bfloat16 [65536, 1152], P(('grp', 'blk')), may hold values from -6 to 6
- log_temp: float32 [1], replicated, may hold values from 2 to 2.7
- bias: float32 [1], replicated, may hold values from -3 to -1
Outputs:
- image_grad: float32 [65536, 1152], P(('grp', 'blk'))
- text_grad: float32 [65536, 1152], P(('grp', 'blk'))
All inputs are finite; a program needn't handle non-finite values.
Results may differ from a plain program's by a relative error of at most 0.0055.
Values may be sent and summed in bfloat16 or wider, within the bound.
A program may use at most 64 MiB of HBM per device.

v0:
```python
import jax
import jax.numpy as jnp
from jax import lax
from jax.sharding import PartitionSpec as P

HOPS = 2


def from_behind(block, axis, distance):
    devices = range(lax.axis_size(axis))
    route = [((i - distance) % len(devices), i) for i in devices]
    return lax.ppermute(block, axis, route)


def unit_rows(values):
    wide = values.astype(jnp.float32)
    norms = jnp.sqrt(jnp.sum(wide * wide, axis=1, keepdims=True) + 1e-06)
    return (wide / norms, norms)


def back_rows(unit, norms, upstream):
    inner = jnp.sum(unit * upstream, axis=1, keepdims=True)
    return (upstream - unit * inner) / norms


def score(own, others, scale, offset):
    return (
        scale
        * lax.dot_general(own, others, (((1,), (1,)), ((), ())), preferred_element_type=jnp.float32)
        + offset
    )


def group_grad(own, others, positive, scale, offset):
    logits = score(own, others, scale, offset)
    sign = jnp.where(positive, jnp.float32(1.0), jnp.float32(-1.0))
    coef = (-sign * jax.nn.sigmoid(-sign * logits) * scale).astype(jnp.bfloat16)
    return jnp.dot(coef, others, preferred_element_type=jnp.float32)


def negative_coef(own, others, scale, offset):
    logits = score(own, others, scale, offset)
    return (jax.nn.sigmoid(logits) * scale).astype(jnp.bfloat16)


def per_device(images, texts, log_temp, bias):
    rows = images.shape[0]
    groups = lax.axis_size("grp")
    group_index = lax.axis_index("grp")
    img_unit, img_norm = unit_rows(images)
    txt_unit, txt_norm = unit_rows(texts)
    img_half = img_unit.astype(jnp.bfloat16)
    txt_half = txt_unit.astype(jnp.bfloat16)
    scale = jnp.exp(log_temp[0])
    offset = bias[0]
    group_txt, group_img = (
        lax.all_gather(txt_half, "grp", axis=0, tiled=True),
        lax.all_gather(img_half, "grp", axis=0, tiled=True),
    )
    diagonal = group_index * rows + lax.iota(jnp.int32, rows)
    columns = lax.iota(jnp.int32, groups * rows)
    positive = diagonal[:, None] == columns[None, :]
    img_grad = group_grad(img_half, group_txt, positive, scale, offset)
    txt_grad = group_grad(txt_half, group_img, positive, scale, offset)
    up_half = txt_half
    down_half = txt_half
    up_sums = jnp.zeros(images.shape, jnp.float32)
    down_sums = up_sums
    for hop in range(HOPS):
        up_half = from_behind(up_half, "blk", 1)
        if hop > 0:
            up_sums = from_behind(up_sums.astype(jnp.bfloat16), "blk", 1).astype(up_sums.dtype)
        coef = negative_coef(img_half, up_half, scale, offset)
        img_grad = img_grad + jnp.dot(coef, up_half, preferred_element_type=jnp.float32)
        up_sums = up_sums + lax.dot_general(
            coef, img_half, (((0,), (0,)), ((), ())), preferred_element_type=jnp.float32
        )
        down_half = from_behind(down_half, "blk", -1)
        if hop > 0:
            down_sums = from_behind(down_sums.astype(jnp.bfloat16), "blk", -1).astype(
                down_sums.dtype
            )
        coef = negative_coef(img_half, down_half, scale, offset)
        img_grad = img_grad + jnp.dot(coef, down_half, preferred_element_type=jnp.float32)
        down_sums = down_sums + lax.dot_general(
            coef, img_half, (((0,), (0,)), ((), ())), preferred_element_type=jnp.float32
        )
    txt_grad = txt_grad + from_behind(up_sums.astype(jnp.bfloat16), "blk", -HOPS).astype(
        up_sums.dtype
    )
    txt_grad = txt_grad + from_behind(down_sums.astype(jnp.bfloat16), "blk", HOPS).astype(
        down_sums.dtype
    )
    return (back_rows(img_unit, img_norm, img_grad), back_rows(txt_unit, txt_norm, txt_grad))


def solution(mesh):
    return jax.shard_map(
        per_device,
        mesh=mesh,
        in_specs=(P(("grp", "blk"), None), P(("grp", "blk"), None), P(), P()),
        out_specs=(P(("grp", "blk"), None), P(("grp", "blk"), None)),
        check_vma=False,
    )
```

profile of v0, /device:TPU:24, one launch (start us, length us, event | category | flops | bytes accessed | tf_op | source)
XLA Modules:
  0.0 248.9 jit_solution(3788742510491085665)
XLA Ops:
  7.2 0.0 all-gather.3.cloned.1.call-start
  7.2 1.1 fusion.50
  8.3 1.8 fusion.66
  10.1 0.0 all-gather.3.cloned.1.call-update
  10.2 0.0 all-gather.5.cloned.1.call-start
  10.2 1.1 fusion.49
  11.3 1.8 fusion.65
  13.1 0.0 all-gather.5.cloned.1.call-update
  13.1 11.4 %collective-permute-start.1 = (bf16[128,1152]{1,0:T(8,128)(2,1)}, bf16[128,1152]{1,0:T(8,128)(2,1)S(1)}, u32[]{:S(2)}, u32[]{:S(2)}) collective-permute-start(bf16[128,1152]{1,0:T(8,128)(2,1)} %fusion.66), channel_id=1, source_target_pairs={{1,0},{2,1},{3,2},{4,3},{5,4},{6,5},{7,6},{8,7},{9,8},{10,9},{11,1... | collective-permute-start | bytes 884744 | tf_op jit(solution)/shard_map/ppermute | solution.py:12
  24.6 1.9 collective-permute-start
  27.9 1.3 collective-permute-done.1
  29.1 1.2 fusion.44
  30.4 0.0 copy-start.3
  30.4 1.2 convolution_convert_fusion
  31.6 5.8 %collective-permute-start.6 = (bf16[128,1152]{1,0:T(8,128)(2,1)S(1)}, bf16[128,1152]{1,0:T(8,128)(2,1)S(1)}, u32[]{:S(2)}, u32[]{:S(2)}) collective-permute-start(bf16[128,1152]{1,0:T(8,128)(2,1)S(1)} %convolution_convert_fusion), channel_id=1, source_target_pairs={{1,0},{2,1},{3,2},{4,3},{5,4},{6,5},{7,6},{8,7},{9,8},{10,9},{11,1... | collective-permute-start | bytes 884744 | tf_op jit(solution)/shard_map/ppermute | solution.py:12
  37.4 1.9 collective-permute-start.3
  39.4 0.0 collective-permute-done
  39.4 1.2 fusion.43
  40.6 0.0 copy-start.4
  40.6 1.2 convolution_convert_fusion.1
  41.9 2.4 collective-permute-start.4
  44.3 1.9 collective-permute-start.2
  46.2 0.0 collective-permute-done.3
  46.2 1.2 fusion.46
  47.5 0.0 copy-done.3
  47.5 0.0 copy-done.4
  47.5 0.0 collective-permute-done.6
  47.5 1.2 add_convert_fusion
  48.7 1.9 collective-permute-start.7
  50.7 4.5 %collective-permute-done.2 = bf16[128,1152]{1,0:T(8,128)(2,1)S(1)} collective-permute-done((bf16[128,1152]{1,0:T(8,128)(2,1)S(1)}, bf16[128,1152]{1,0:T(8,128)(2,1)S(1)}, u32[]{:S(2)}, u32[]{:S(2)}) %collective-permute-start.2) | collective-permute-done | bytes 294944 | tf_op jit(solution)/shard_map/ppermute | solution.py:12
  55.2 0.0 copy-done
  55.2 0.3 fusion.45
  55.5 0.0 collective-permute-done.4
  55.5 0.3 add_convert_fusion.1
  55.8 1.9 collective-permute-start.5
  57.7 0.2 fusion.69
  57.9 66.8 %all-gather.3.cloned.1.call-done = bf16[2048,1152]{1,0:T(8,128)(2,1)} async-done(((bf16[128,1152]{1,0:T(8,128)(2,1)}), bf16[2048,1152]{1,0:T(8,128)(2,1)}) %all-gather.3.cloned.1.call-update) | async-done | bytes 4718608 | tf_op jit(solution)/shard_map/all_gather | solution.py:57
  124.7 6.2 %fusion.47 = f32[128,1152]{1,0:T(8,128)S(1)} fusion(bf16[2048,1152]{1,0:T(8,128)(2,1)} %all-gather.3.cloned.1.call-done, bf16[128,1152]{1,0:T(8,128)(2,1)S(1)} %copy-done, f32[]{:T(128)} %bitcast.31, f32[]{:T(128)} %bitcast, s32[128]{0:T(128)S(1)} %iota_add_fusion), kind=kOutput, calls=%fused_computation.60 | convolution fusion | flops 1211105280 | bytes 5603848 | tf_op jit(solution)/shard_map/dot_general | solution.py:38
  130.9 0.0 copy-start.1
  130.9 1.0 convolution_add_fusion.2
  132.0 1.0 convolution_add_fusion.1
  133.0 1.3 multiply_reduce_fusion.1
  134.3 1.0 subtract_divide_fusion.1
  135.3 0.0 collective-permute-done.7
  135.3 0.0 collective-permute-done.5
  135.3 99.3 %all-gather.5.cloned.1.call-done = bf16[2048,1152]{1,0:T(8,128)(2,1)} async-done(((bf16[128,1152]{1,0:T(8,128)(2,1)}), bf16[2048,1152]{1,0:T(8,128)(2,1)}) %all-gather.5.cloned.1.call-update) | async-done | bytes 4718608 | tf_op jit(solution)/shard_map/all_gather | solution.py:58
  234.7 6.3 %multiply_reduce_fusion = (f32[128]{0:T(128)S(1)}, f32[128,1152]{1,0:T(8,128)S(1)}) fusion(bf16[128,1152]{1,0:T(8,128)(2,1)S(1)} %collective-permute-done.7, bf16[128,1152]{1,0:T(8,128)(2,1)S(1)} %collective-permute-done.5, f32[128]{0:T(128)S(1)} %add_sqrt_fusion, bf16[128,1152]{1,0:T(8,128)(2,1)S(1)} %copy-done.1, ...), kind=kOutput, calls=%fused_computation.69 | convolution fusion | flops 1212727168 | bytes 6194696 | tf_op jit(solution)/shard_map/dot_general | solution.py:38
  241.0 1.0 subtract_divide_fusion
  (11 shorter events, 0.0 us)
Async XLA Ops:
  7.2 117.6 %all-gather.3.cloned.1.call-start = ((), (), s32[]{:S(2)}) async-start(), calls=%async_computation | async-start | bytes 5013504 | tf_op jit(solution)/shard_map/all_gather | solution.py:57
  10.2 224.5 %all-gather.5.cloned.1.call-start = ((), (), s32[]{:S(2)}) async-start(), calls=%async_computation.1 | async-start | bytes 5013504 | tf_op jit(solution)/shard_map/all_gather | solution.py:58
  13.1 42.1 %copy-start = (bf16[128,1152]{1,0:T(8,128)(2,1)S(1)}, bf16[128,1152]{1,0:T(8,128)(2,1)}, u32[]{:S(2)}) copy-start(bf16[128,1152]{1,0:T(8,128)(2,1)} %fusion.65) | copy-start | bytes 884740
  13.1 16.0 %collective-permute-start.1 = (bf16[128,1152]{1,0:T(8,128)(2,1)}, bf16[128,1152]{1,0:T(8,128)(2,1)S(1)}, u32[]{:S(2)}, u32[]{:S(2)}) collective-permute-start(bf16[128,1152]{1,0:T(8,128)(2,1)} %fusion.66), channel_id=1, source_target_pairs={{1,0},{2,1},{3,2},{4,3},{5,4},{6,5},{7,6},{8,7},{9,8},{10,9},{11,1... | collective-permute-start | bytes 884744 | tf_op jit(solution)/shard_map/ppermute | solution.py:12
  24.6 14.8 %collective-permute-start = (bf16[128,1152]{1,0:T(8,128)(2,1)}, bf16[128,1152]{1,0:T(8,128)(2,1)S(1)}, u32[]{:S(2)}, u32[]{:S(2)}) collective-permute-start(bf16[128,1152]{1,0:T(8,128)(2,1)} %fusion.66), channel_id=1, source_target_pairs={{31,0},{0,1},{1,2},{2,3},{3,4},{4,5},{5,6},{6,7},{7,8},{8,9},{9,10... | collective-permute-start | bytes 884744 | tf_op jit(solution)/shard_map/ppermute | solution.py:12
  30.4 17.1 %copy-start.3 = (bf16[128,128]{1,0:T(8,128)(2,1)}, bf16[128,128]{1,0:T(8,128)(2,1)S(1)}, u32[]{:S(2)}) copy-start(bf16[128,128]{1,0:T(8,128)(2,1)S(1)} %fusion.44) | copy-start | bytes 98308
  31.6 15.9 %collective-permute-start.6 = (bf16[128,1152]{1,0:T(8,128)(2,1)S(1)}, bf16[128,1152]{1,0:T(8,128)(2,1)S(1)}, u32[]{:S(2)}, u32[]{:S(2)}) collective-permute-start(bf16[128,1152]{1,0:T(8,128)(2,1)S(1)} %convolution_convert_fusion), channel_id=1, source_target_pairs={{1,0},{2,1},{3,2},{4,3},{5,4},{6,5},{7,6},{8,7},{9,8},{10,9},{11,1... | collective-permute-start | bytes 884744 | tf_op jit(solution)/shard_map/ppermute | solution.py:12
  37.4 8.8 %collective-permute-start.3 = (bf16[128,1152]{1,0:T(8,128)(2,1)S(1)}, bf16[128,1152]{1,0:T(8,128)(2,1)S(1)}, u32[]{:S(2)}, u32[]{:S(2)}) collective-permute-start(bf16[128,1152]{1,0:T(8,128)(2,1)S(1)} %collective-permute-done.1), channel_id=1, source_target_pairs={{1,0},{2,1},{3,2},{4,3},{5,4},{6,5},{7,6},{8,7},{9,8},{10,9},{11,1... | collective-permute-start | bytes 884744 | tf_op jit(solution)/shard_map/ppermute | solution.py:12
  40.6 6.9 %copy-start.4 = (bf16[128,128]{1,0:T(8,128)(2,1)}, bf16[128,128]{1,0:T(8,128)(2,1)S(1)}, u32[]{:S(2)}) copy-start(bf16[128,128]{1,0:T(8,128)(2,1)S(1)} %fusion.43) | copy-start | bytes 98308
  41.9 13.6 %collective-permute-start.4 = (bf16[128,1152]{1,0:T(8,128)(2,1)S(1)}, bf16[128,1152]{1,0:T(8,128)(2,1)S(1)}, u32[]{:S(2)}, u32[]{:S(2)}) collective-permute-start(bf16[128,1152]{1,0:T(8,128)(2,1)S(1)} %convolution_convert_fusion.1), channel_id=1, source_target_pairs={{31,0},{0,1},{1,2},{2,3},{3,4},{4,5},{5,6},{6,7},{7,8},{8,9},{9,10... | collective-permute-start | bytes 884744 | tf_op jit(solution)/shard_map/ppermute | solution.py:12
  44.3 10.9 %collective-permute-start.2 = (bf16[128,1152]{1,0:T(8,128)(2,1)S(1)}, bf16[128,1152]{1,0:T(8,128)(2,1)S(1)}, u32[]{:S(2)}, u32[]{:S(2)}) collective-permute-start(bf16[128,1152]{1,0:T(8,128)(2,1)S(1)} %collective-permute-done), channel_id=1, source_target_pairs={{31,0},{0,1},{1,2},{2,3},{3,4},{4,5},{5,6},{6,7},{7,8},{8,9},{9,10... | collective-permute-start | bytes 884744 | tf_op jit(solution)/shard_map/ppermute | solution.py:12
  48.7 86.6 %collective-permute-start.7 = (bf16[128,1152]{1,0:T(8,128)(2,1)S(1)}, bf16[128,1152]{1,0:T(8,128)(2,1)S(1)}, u32[]{:S(2)}, u32[]{:S(2)}) collective-permute-start(bf16[128,1152]{1,0:T(8,128)(2,1)S(1)} %add_convert_fusion), channel_id=1, source_target_pairs={{30,0},{31,1},{0,2},{1,3},{2,4},{3,5},{4,6},{5,7},{6,8},{7,9},{8,1... | collective-permute-start | bytes 884744 | tf_op jit(solution)/shard_map/ppermute | solution.py:12
  55.2 2.5 %copy-start.6 = (bf16[128,1152]{1,0:T(8,128)(2,1)}, bf16[128,1152]{1,0:T(8,128)(2,1)S(1)}, u32[]{:S(2)}) copy-start(bf16[128,1152]{1,0:T(8,128)(2,1)S(1)} %collective-permute-done.2) | copy-start | bytes 884740
  55.5 2.2 copy-start.5
  55.8 79.6 %collective-permute-start.5 = (bf16[128,1152]{1,0:T(8,128)(2,1)S(1)}, bf16[128,1152]{1,0:T(8,128)(2,1)S(1)}, u32[]{:S(2)}, u32[]{:S(2)}) collective-permute-start(bf16[128,1152]{1,0:T(8,128)(2,1)S(1)} %add_convert_fusion.1), channel_id=1, source_target_pairs={{2,0},{3,1},{4,2},{5,3},{6,4},{7,5},{8,6},{9,7},{10,8},{11,9},{12,... | collective-permute-start | bytes 884744 | tf_op jit(solution)/shard_map/ppermute | solution.py:12
  124.7 8.2 %copy-start.2 = (bf16[128,1152]{1,0:T(8,128)(2,1)S(1)}, bf16[128,1152]{1,0:T(8,128)(2,1)}, u32[]{:S(2)}) copy-start(bf16[128,1152]{1,0:T(8,128)(2,1)} %param.4) | copy-start | bytes 884740
  130.9 103.7 %copy-start.1 = (bf16[128,1152]{1,0:T(8,128)(2,1)S(1)}, bf16[128,1152]{1,0:T(8,128)(2,1)}, u32[]{:S(2)}) copy-start(bf16[128,1152]{1,0:T(8,128)(2,1)} %param.5) | copy-start | bytes 884740
Sparse Core Ops, SparseCore 0:
  11.7 112.9 all-gather.2
  128.5 106.1 all-gather.4
where the time goes:
time: 250 us; the launch traced here: 249 us
  waiting for transfers between devices  172 us (69%)
  starting transfers between devices  29.3 us (12%)
  matrix products  24 us (10%)
  between operations  15.6 us (6%)
  other arithmetic  7.89 us (3%)
    all_gather x1, waiting for transfers between devices, per_device(): lax.all_gather(img_half, 'grp', axis=0, tiled=True)  99.3 us
    all_gather x1, waiting for transfers between devices, per_device(): lax.all_gather(txt_half, 'grp', axis=0, tiled=True)  66.8 us
    ppermute x8, starting transfers between devices, from_behind(): return lax.ppermute(block, axis, route)  29.3 us
    dot_general x2, matrix products, group_grad(): return jnp.dot(coef, others, preferred_element_type=jnp.float32)  12.5 us
    ppermute x8, waiting for transfers between devices, from_behind(): return lax.ppermute(block, axis, route)  5.8 us
  transfers between devices with their start and end apart: 10, of which 4 were waited for; matrix products, arithmetic and copies ran while one was open for 9% of the time, Pallas kernels for 0%

commit v1 on v0

v1 whole, which is shorter than its diff:
```python
import jax
import jax.numpy as jnp
from jax import lax
from jax.experimental import pallas as pl
from jax.experimental.pallas import tpu as pltpu
from jax.sharding import PartitionSpec as P

MESH = pl.DeviceIdType.MESH
ROWS = 128
D = 1152
HALF = 64
RING = 8
OFFSETS = (1, -1, 2, -2)

F32 = jnp.float32
BF16 = jnp.bfloat16


def dot_nt(a, b):
    return lax.dot_general(a, b, (((1,), (1,)), ((), ())), preferred_element_type=F32)


def dot_nn(a, b):
    return jnp.dot(a, b, preferred_element_type=F32)


def rows_norm(values):
    wide = values.astype(F32)
    return jnp.sqrt(jnp.sum(wide * wide, axis=1, keepdims=True) + 1e-06)


def back_rows(values, norms, upstream):
    rcp = 1.0 / norms
    unit = values.astype(F32) * rcp
    inner = jnp.sum(unit * upstream, axis=1, keepdims=True)
    return (upstream - unit * inner) * rcp


def kernel(
    temp_ref,
    bias_ref,
    img_ref,
    txt_ref,
    gi_ref,
    gt_ref,
    own_txt,
    imgs,
    ring,
    far,
    near_img,
    near_txt,
    img_acc,
    txt_acc,
    part,
    part_far,
    out_l,
    out_r,
    in_l,
    in_r,
    img_out,
    img_in,
    norms,
    sems,
):
    g = lax.axis_index("grp")
    b = lax.axis_index("blk")
    n_grp = lax.axis_size("grp")
    n_blk = lax.axis_size("blk")
    fore = ((g + 2) % n_grp, b)
    back = ((g + n_grp - 2) % n_grp, b)
    mate = (g + 1 - 2 * (g % 2), b)
    near = [(g, (b + n_blk + o) % n_blk) for o in OFFSETS]

    barrier = pltpu.get_barrier_semaphore()
    for dev in [fore, back, mate] + near:
        pl.semaphore_signal(barrier, inc=1, device_id=dev, device_id_type=MESH)

    scale = jnp.exp(jnp.full((1, 1), temp_ref[0], F32))
    offset = bias_ref[0]

    pending = []
    count = [0]

    def send(src, dst, dev):
        i = count[0]
        count[0] += 1
        copy = pltpu.make_async_remote_copy(
            src_ref=src,
            dst_ref=dst,
            send_sem=sems.at[0, i],
            recv_sem=sems.at[1, i],
            device_id=dev,
            device_id_type=MESH,
        )
        copy.start()
        pending.append(copy)
        return copy

    def half(h):
        return pl.ds(h * HALF, HALF)

    tn = rows_norm(txt_ref[...])
    norms[1] = tn
    own_txt[...] = (txt_ref[...].astype(F32) * (1.0 / tn)).astype(BF16)
    pl.semaphore_wait(barrier, 7)

    gather_f = {}
    gather_b = {}
    for h in range(2):
        gather_f[1, h] = send(own_txt.at[half(h)], ring.at[0, half(h)], fore)
        gather_b[1, h] = send(own_txt.at[half(h)], ring.at[0, pl.ds(ROWS + h * HALF, HALF)], back)

    im = rows_norm(img_ref[...])
    norms[0] = im
    imgs[0:ROWS] = (img_ref[...].astype(F32) * (1.0 / im)).astype(BF16)
    mate_copy = send(imgs.at[pl.ds(0, ROWS)], imgs.at[pl.ds(ROWS, ROWS)], mate)

    def forward(k):
        for h in range(2):
            f = (k + 1, h)
            gather_f[k, h].wait_recv()
            if k < 3:
                gather_f[f] = send(ring.at[k - 1, half(h)], ring.at[k, half(h)], fore)
            elif h == 0:
                gather_f[f] = send(ring.at[k - 1, half(0)], far.at[half(0)], fore)
            gather_b[k, h].wait_recv()
            up = pl.ds(ROWS + h * HALF, HALF)
            if k < 3:
                gather_b[f] = send(ring.at[k - 1, up], ring.at[k, up], back)
            elif h == 1:
                gather_b[f] = send(ring.at[k - 1, up], far.at[half(1)], back)

    def negative(logits):
        return (jax.nn.sigmoid(logits) * scale).astype(BF16)

    def score(a, c):
        return scale * dot_nt(a, c) + offset

    def ring_step(k):
        texts = ring[k - 1]
        pair = imgs[...]
        coef = negative(score(pair, texts))
        img_acc[...] += dot_nn(coef, texts)
        part[k - 1] = dot_nn(coef.T, pair)

    forward(1)
    forward(2)
    mate_copy.wait_recv()

    near_copies = []
    for i, dev in enumerate(near):
        near_copies.append(send(imgs.at[pl.ds(0, ROWS)], near_img.at[pl.ds(i * ROWS, ROWS)], dev))
        near_copies.append(send(own_txt, near_txt.at[pl.ds(i * ROWS, ROWS)], dev))

    texts = own_txt[...]
    pair = imgs[...]
    logits = score(pair, texts)
    same = lax.broadcasted_iota(jnp.int32, logits.shape, 0) == lax.broadcasted_iota(
        jnp.int32, logits.shape, 1
    )
    sign = jnp.where(same, jnp.float32(1.0), jnp.float32(-1.0))
    coef = (-sign * jax.nn.sigmoid(-sign * logits) * scale).astype(BF16)
    img_acc[...] = dot_nn(coef, texts)
    txt_acc[...] = dot_nn(coef.T, pair)
    ring_step(1)
    ring_step(2)

    forward(3)
    ring_step(3)

    sums_l = {}
    sums_r = {}

    def give_l(k, h, value):
        out_l[k - 1, half(h)] = value.astype(BF16)
        sums_l[k - 1, h] = send(out_l.at[k - 1, half(h)], in_l.at[k - 1, half(h)], back)

    def give_r(k, h, value):
        out_r[k - 1, half(h)] = value.astype(BF16)
        sums_r[k - 1, h] = send(out_r.at[k - 1, half(h)], in_r.at[k - 1, half(h)], fore)

    def mine_l(k, h):
        return part[k - 1, half(h)]

    def mine_r(k, h):
        return part[k - 1, pl.ds(ROWS + h * HALF, HALF)]

    give_l(3, 1, mine_l(3, 1))
    give_r(3, 0, mine_r(3, 0))

    gather_f[4, 0].wait_recv()
    gather_b[4, 1].wait_recv()
    texts = far[...]
    pair = imgs[...]
    coef = negative(score(pair, texts))
    part_far[...] = dot_nn(coef.T, pair)
    give_l(4, 0, part_far[half(0)])
    give_r(4, 1, part_far[half(1)])
    img_acc[...] += dot_nn(coef, texts)
    img_out[...] = img_acc[ROWS : 2 * ROWS].astype(BF16)
    img_back = send(img_out, img_in, mate)

    def relay(k, h):
        sums_l[k, h].wait_recv()
        give_l(k, h, mine_l(k, h) + in_l[k, half(h)].astype(F32))
        q = 1 - h
        sums_r[k, q].wait_recv()
        give_r(k, q, mine_r(k, q) + in_r[k, half(q)].astype(F32))

    relay(2, 1)
    relay(3, 0)
    relay(1, 1)
    relay(2, 0)

    for copy in near_copies:
        copy.wait_recv()
    texts = near_txt[...]
    coef = negative(score(imgs[0:ROWS], texts))
    img_acc[0:ROWS] += dot_nn(coef, texts)
    relay(1, 0)

    others = near_img[...]
    coef = negative(score(own_txt[...], others))
    txt_acc[...] += dot_nn(coef, others)

    img_back.wait_recv()
    gi_ref[...] = back_rows(
        img_ref[...], norms[0], img_acc[0:ROWS] + img_in[...].astype(F32)
    )

    sums_l[0, 1].wait_recv()
    sums_r[0, 0].wait_recv()
    sums_l[0, 0].wait_recv()
    sums_r[0, 1].wait_recv()
    gt_ref[...] = back_rows(
        txt_ref[...],
        norms[1],
        txt_acc[...] + in_l[0].astype(F32) + in_r[0].astype(F32),
    )
    for copy in pending:
        copy.wait_send()


def per_device(images, texts, log_temp, bias):
    vmem = pl.BlockSpec(memory_space=pltpu.VMEM)
    smem = pl.BlockSpec(memory_space=pltpu.SMEM)
    out = jax.ShapeDtypeStruct((ROWS, D), F32)
    return pl.pallas_call(
        kernel,
        out_shape=(out, out),
        in_specs=[smem, smem, vmem, vmem],
        out_specs=(vmem, vmem),
        scratch_shapes=[
            pltpu.VMEM((ROWS, D), BF16),
            pltpu.VMEM((2 * ROWS, D), BF16),
            pltpu.VMEM((3, 2 * ROWS, D), BF16),
            pltpu.VMEM((ROWS, D), BF16),
            pltpu.VMEM((4 * ROWS, D), BF16),
            pltpu.VMEM((4 * ROWS, D), BF16),
            pltpu.VMEM((2 * ROWS, D), F32),
            pltpu.VMEM((ROWS, D), F32),
            pltpu.VMEM((3, 2 * ROWS, D), F32),
            pltpu.VMEM((ROWS, D), F32),
            pltpu.VMEM((4, ROWS, D), BF16),
            pltpu.VMEM((4, ROWS, D), BF16),
            pltpu.VMEM((4, ROWS, D), BF16),
            pltpu.VMEM((4, ROWS, D), BF16),
            pltpu.VMEM((ROWS, D), BF16),
            pltpu.VMEM((ROWS, D), BF16),
            pltpu.VMEM((2, ROWS, 1), F32),
            pltpu.SemaphoreType.DMA((2, 40)),
        ],
        compiler_params=pltpu.CompilerParams(
            collective_id=0, has_side_effects=True, vmem_limit_bytes=40 * 1024 * 1024
        ),
        cost_estimate=pl.CostEstimate(
            flops=2_600_000_000, bytes_accessed=2_000_000, transcendentals=500_000
        ),
    )(log_temp, bias, images, texts)


def solution(mesh):
    return jax.shard_map(
        per_device,
        mesh=mesh,
        in_specs=(P(("grp", "blk"), None), P(("grp", "blk"), None), P(), P()),
        out_specs=(P(("grp", "blk"), None), P(("grp", "blk"), None)),
        check_vma=False,
    )
```

time: 250 us -> 70 us (0.28)
  the two profiles are of different devices: /device:TPU:24 before, /device:TPU:4 now
where the time goes in v1:
time: 70 us; the launch traced here: 69.8 us
  Pallas kernels  64.3 us (92%)
  local copies, waits for them, and re-layouts  3.55 us (5%)
  between operations  1.94 us (3%)
    pallas_call x1, Pallas kernels, per_device(): pl.pallas_call(kernel, out_shape=(out, out), in_specs=[smem, smem, vmem,...  64.3 us
    unnamed x6, local copies, waits for them, and re-layouts  3.55 us

profile of v1, /device:TPU:4, one launch (start us, length us, event | category | flops | bytes accessed | tf_op | source)
XLA Modules:
  0.0 69.8 jit_solution(14723992418527427800)
XLA Ops:
  1.9 0.0 copy-start
  1.9 1.0 %copy-done = bf16[128,1152]{1,0:T(8,128)(2,1)S(1)} copy-done((bf16[128,1152]{1,0:T(8,128)(2,1)S(1)}, bf16[128,1152]{1,0:T(8,128)(2,1)}, u32[]{:S(2)}) %copy-start) | copy-done | bytes 294936
  2.9 0.0 copy-start.1
  2.9 1.0 %copy-done.1 = bf16[128,1152]{1,0:T(8,128)(2,1)S(1)} copy-done((bf16[128,1152]{1,0:T(8,128)(2,1)S(1)}, bf16[128,1152]{1,0:T(8,128)(2,1)}, u32[]{:S(2)}) %copy-start.1) | copy-done | bytes 294936
  3.8 64.3 %shard_map.59 = (f32[128,1152]{1,0:T(8,128)S(1)}, f32[128,1152]{1,0:T(8,128)S(1)}) custom-call(f32[1]{0:T(128)S(6)} %copy.8.temp_ref, f32[1]{0:T(128)S(6)} %copy.9.bias_ref, bf16[128,1152]{1,0:T(8,128)(2,1)S(1)} %copy-done, bf16[128,1152]{1,0:T(8,128)(2,1)S(1)} %copy-done.1), custom_call_target="tpu_custom_call" | custom-call | flops 2600000000 | bytes 2000000 | tf_op jit(solution)/shard_map/pallas_call | solution.py:248
  68.2 0.8 %copy.10 = f32[128,1152]{1,0:T(8,128)} copy(f32[128,1152]{1,0:T(8,128)S(1)} %get-tuple-element.4) | data formatting | bytes 1179648
  69.0 0.8 %copy.11 = f32[128,1152]{1,0:T(8,128)} copy(f32[128,1152]{1,0:T(8,128)S(1)} %get-tuple-element.5) | data formatting | bytes 1179648
Async XLA Ops:
  1.9 1.0 %copy-start = (bf16[128,1152]{1,0:T(8,128)(2,1)S(1)}, bf16[128,1152]{1,0:T(8,128)(2,1)}, u32[]{:S(2)}) copy-start(bf16[128,1152]{1,0:T(8,128)(2,1)} %img_ref.1) | copy-start | bytes 884740
  2.9 1.0 %copy-start.1 = (bf16[128,1152]{1,0:T(8,128)(2,1)S(1)}, bf16[128,1152]{1,0:T(8,128)(2,1)}, u32[]{:S(2)}) copy-start(bf16[128,1152]{1,0:T(8,128)(2,1)} %txt_ref.1) | copy-start | bytes 884740

commit v2 on v1

v2 whole, which is shorter than its diff:
```python
import jax
import jax.numpy as jnp
from jax import lax
from jax.experimental import pallas as pl
from jax.experimental.pallas import tpu as pltpu
from jax.sharding import PartitionSpec as P

MESH = pl.DeviceIdType.MESH
ROWS = 128
D = 1152
C = 4
H = C // 2
R = ROWS // C
OFFSETS = (1, -1, 2, -2)

F32 = jnp.float32
BF16 = jnp.bfloat16


def dot_nt(a, b):
    return lax.dot_general(a, b, (((1,), (1,)), ((), ())), preferred_element_type=F32)


def dot_nn(a, b):
    return jnp.dot(a, b, preferred_element_type=F32)


def rows_norm(values):
    wide = values.astype(F32)
    return jnp.sqrt(jnp.sum(wide * wide, axis=1, keepdims=True) + 1e-06)


def unit_half(values):
    return (values.astype(F32) * (1.0 / rows_norm(values))).astype(BF16)


def back_rows(values, norms, upstream):
    rcp = 1.0 / norms
    unit = values.astype(F32) * rcp
    inner = jnp.sum(unit * upstream, axis=1, keepdims=True)
    return (upstream - unit * inner) * rcp


def rank(b):
    return jnp.where((b // 2) % 8 == 0, 0, 1000) + (b % 2) * 100 + b


def chunk(c):
    return pl.ds(c * R, R)


def kernel(
    temp_ref,
    bias_ref,
    img_ref,
    txt_ref,
    gi_ref,
    gt_ref,
    img_v,
    txt_v,
    own_txt,
    mate_raw,
    imgs,
    ring,
    ring_half,
    far,
    near_img,
    near_txt,
    img_acc,
    txt_acc,
    part,
    part_far,
    out_l,
    out_r,
    in_l,
    in_r,
    img_out,
    img_in,
    norms,
    local_sems,
    sems,
    ready,
):
    g = lax.axis_index("grp")
    b = lax.axis_index("blk")
    n_grp = lax.axis_size("grp")
    n_blk = lax.axis_size("blk")
    fore = ((g + 2) % n_grp, b)
    back = ((g + n_grp - 2) % n_grp, b)
    mate = (g + 1 - 2 * (g % 2), b)
    near_blk = [(b + n_blk + o) % n_blk for o in OFFSETS]
    near = [(g, n) for n in near_blk]
    earlier = [rank(n) < rank(b) for n in near_blk]

    loads = []
    for i, (src, dst) in enumerate(((txt_ref, txt_v), (img_ref, img_v))):
        load = pltpu.make_async_copy(src, dst, local_sems.at[i])
        load.start()
        loads.append(load)

    barrier = pltpu.get_barrier_semaphore()
    for dev in (fore, back, mate):
        pl.semaphore_signal(barrier, inc=1, device_id=dev, device_id_type=MESH)
    greeted = 3
    for dev, known in zip(near, earlier):

        @pl.when(jnp.logical_not(known))
        def _():
            pl.semaphore_signal(barrier, inc=1, device_id=dev, device_id_type=MESH)

        greeted = greeted + known.astype(jnp.int32)
    pl.semaphore_wait(barrier, greeted)

    pending = []
    count = [0]

    def prepare(src, dst, dev):
        i = count[0]
        count[0] += 1
        copy = pltpu.make_async_remote_copy(
            src_ref=src,
            dst_ref=dst,
            send_sem=sems.at[0, i],
            recv_sem=sems.at[1, i],
            device_id=dev,
            device_id_type=MESH,
        )
        pending.append(copy)
        return copy

    def send(src, dst, dev):
        copy = prepare(src, dst, dev)
        copy.start()
        return copy

    def upper(c):
        return pl.ds(ROWS + c * R, R)

    gather_f = {}
    gather_b = {}
    for c in range(C):
        d = C - 1 - c
        gather_f[1, c] = send(txt_ref.at[chunk(c)], ring.at[0, chunk(c)], fore)
        gather_b[1, d] = send(txt_ref.at[chunk(d)], ring.at[0, upper(d)], back)
    mate_copy = send(img_ref, mate_raw, mate)
    for dev, known in zip(near, earlier):

        @pl.when(known)
        def _():
            pl.semaphore_signal(ready, inc=1, device_id=dev, device_id_type=MESH)

    for load in loads:
        load.wait()
    norms[1] = rows_norm(txt_v[...])
    own_txt[...] = (txt_v[...].astype(F32) * (1.0 / norms[1])).astype(BF16)
    norms[0] = rows_norm(img_v[...])
    imgs[0:ROWS] = (img_v[...].astype(F32) * (1.0 / norms[0])).astype(BF16)
    scale = jnp.exp(temp_ref[...])
    offset = bias_ref[...]

    near_copies = []
    for i, dev in enumerate(near):
        rows = pl.ds(i * ROWS, ROWS)
        near_copies.append(prepare(imgs.at[pl.ds(0, ROWS)], near_img.at[rows], dev))
        near_copies.append(prepare(own_txt, near_txt.at[rows], dev))

    def send_near(which):
        for i in range(len(OFFSETS)):

            @pl.when(which[i])
            def _():
                near_copies[2 * i].start()
                near_copies[2 * i + 1].start()

    def forward(k, c):
        d = C - 1 - c
        gather_f[k, c].wait_recv()
        if k < 3:
            gather_f[k + 1, c] = send(ring.at[k - 1, chunk(c)], ring.at[k, chunk(c)], fore)
        elif c < H:
            gather_f[4, c] = send(ring.at[k - 1, chunk(c)], far.at[chunk(c)], fore)
        gather_b[k, d].wait_recv()
        if k < 3:
            gather_b[k + 1, d] = send(ring.at[k - 1, upper(d)], ring.at[k, upper(d)], back)
        elif d >= H:
            gather_b[4, d] = send(ring.at[k - 1, upper(d)], far.at[chunk(d)], back)

    def negative(logits):
        return (jax.nn.sigmoid(logits) * scale).astype(BF16)

    def score(a, c):
        return scale * dot_nt(a, c) + offset

    def ring_step(k):
        ring_half[...] = unit_half(ring[k - 1])
        texts = ring_half[...]
        pair = imgs[...]
        coef = negative(score(pair, texts))
        part[k - 1] = dot_nn(coef.T, pair)
        img_acc[...] += dot_nn(coef, texts)

    def own_step():
        texts = own_txt[...]
        pair = imgs[...]
        logits = score(pair, texts)
        same = lax.broadcasted_iota(jnp.int32, logits.shape, 0) == lax.broadcasted_iota(
            jnp.int32, logits.shape, 1
        )
        sign = jnp.where(same, jnp.float32(1.0), jnp.float32(-1.0))
        coef = (-sign * jax.nn.sigmoid(-sign * logits) * scale).astype(BF16)
        img_acc[...] = dot_nn(coef, texts)
        txt_acc[...] = dot_nn(coef.T, pair)

    for c in range(C):
        forward(1, c)
    for c in range(H):
        forward(2, c)
    mate_copy.wait_recv()
    send_near(earlier)
    imgs[ROWS : 2 * ROWS] = unit_half(mate_raw[...])
    for c in range(H, C):
        forward(2, c)
    own_step()
    forward(3, 0)
    ring_step(1)
    forward(3, 1)
    ring_step(2)
    for c in range(H, C):
        forward(3, c)
    ring_step(3)

    sums_l = {}
    sums_r = {}

    def give_l(k, c, value):
        out_l[k - 1, chunk(c)] = value.astype(BF16)
        sums_l[k - 1, c] = send(out_l.at[k - 1, chunk(c)], in_l.at[k - 1, chunk(c)], back)

    def give_r(k, c, value):
        out_r[k - 1, chunk(c)] = value.astype(BF16)
        sums_r[k - 1, c] = send(out_r.at[k - 1, chunk(c)], in_r.at[k - 1, chunk(c)], fore)

    for c in range(H, C):
        d = C - 1 - c
        give_l(3, c, part[2, chunk(c)])
        give_r(3, d, part[2, upper(d)])

    answers = 3 + len(near) - greeted

    @pl.when(answers > 0)
    def _():
        pl.semaphore_wait(ready, answers)

    send_near([jnp.logical_not(known) for known in earlier])

    for c in range(H):
        gather_f[4, c].wait_recv()
        gather_b[4, C - 1 - c].wait_recv()
    texts = unit_half(far[...])
    pair = imgs[...]
    coef = negative(score(pair, texts))
    part_far[...] = dot_nn(coef.T, pair)
    for c in range(H):
        d = C - 1 - c
        give_l(4, c, part_far[chunk(c)])
        give_r(4, d, part_far[chunk(d)])
    img_acc[...] += dot_nn(coef, texts)
    img_out[...] = img_acc[ROWS : 2 * ROWS].astype(BF16)
    img_back = send(img_out, img_in, mate)

    def relay(k, c):
        d = C - 1 - c
        sums_l[k, c].wait_recv()
        give_l(k, c, part[k - 1, chunk(c)] + in_l[k, chunk(c)].astype(F32))
        sums_r[k, d].wait_recv()
        give_r(k, d, part[k - 1, upper(d)] + in_r[k, chunk(d)].astype(F32))

    for c in range(H, C):
        relay(2, c)
    for c in range(H):
        relay(3, c)
    for c in range(H, C):
        relay(1, c)
    for c in range(H):
        relay(2, c)

    for copy in near_copies:
        copy.wait_recv()
    texts = near_txt[...]
    coef = negative(score(imgs[0:ROWS], texts))
    img_acc[0:ROWS] += dot_nn(coef, texts)

    for c in range(H):
        relay(1, c)

    others = near_img[...]
    coef = negative(score(own_txt[...], others))
    txt_acc[...] += dot_nn(coef, others)
    img_back.wait_recv()
    gi_ref[...] = back_rows(
        img_v[...], norms[0], img_acc[0:ROWS] + img_in[...].astype(F32)
    )

    for c in range(H, C):
        d = C - 1 - c
        sums_l[0, c].wait_recv()
        sums_r[0, d].wait_recv()
        txt_acc[chunk(c)] += in_l[0, chunk(c)].astype(F32)
        txt_acc[chunk(d)] += in_r[0, chunk(d)].astype(F32)
    for c in range(H):
        d = C - 1 - c
        sums_l[0, c].wait_recv()
        gt_ref[chunk(c)] = back_rows(
            txt_v[chunk(c)],
            norms[1, chunk(c)],
            txt_acc[chunk(c)] + in_l[0, chunk(c)].astype(F32),
        )
        sums_r[0, d].wait_recv()
        gt_ref[chunk(d)] = back_rows(
            txt_v[chunk(d)],
            norms[1, chunk(d)],
            txt_acc[chunk(d)] + in_r[0, chunk(d)].astype(F32),
        )
    for copy in pending:
        copy.wait_send()


def store(gi_ref, gt_ref, oi_ref, ot_ref, sems):
    copies = [
        pltpu.make_async_copy(gi_ref, oi_ref, sems.at[0]),
        pltpu.make_async_copy(gt_ref, ot_ref, sems.at[1]),
    ]
    for copy in copies:
        copy.start()
    for copy in copies:
        copy.wait()


def per_device(images, texts, log_temp, bias):
    vmem = pl.BlockSpec(memory_space=pltpu.VMEM)
    hbm = pl.BlockSpec(memory_space=pltpu.HBM)
    out = jax.ShapeDtypeStruct((ROWS, D), F32)
    sums = pl.pallas_call(
        kernel,
        out_shape=(out, out),
        in_specs=[vmem] * 2 + [hbm] * 2,
        out_specs=(vmem, vmem),
        scratch_shapes=[
            pltpu.VMEM((ROWS, D), BF16),
            pltpu.VMEM((ROWS, D), BF16),
            pltpu.VMEM((ROWS, D), BF16),
            pltpu.VMEM((ROWS, D), BF16),
            pltpu.VMEM((2 * ROWS, D), BF16),
            pltpu.VMEM((3, 2 * ROWS, D), BF16),
            pltpu.VMEM((2 * ROWS, D), BF16),
            pltpu.VMEM((ROWS, D), BF16),
            pltpu.VMEM((4 * ROWS, D), BF16),
            pltpu.VMEM((4 * ROWS, D), BF16),
            pltpu.VMEM((2 * ROWS, D), F32),
            pltpu.VMEM((ROWS, D), F32),
            pltpu.VMEM((3, 2 * ROWS, D), F32),
            pltpu.VMEM((ROWS, D), F32),
            pltpu.VMEM((4, ROWS, D), BF16),
            pltpu.VMEM((4, ROWS, D), BF16),
            pltpu.VMEM((4, ROWS, D), BF16),
            pltpu.VMEM((4, ROWS, D), BF16),
            pltpu.VMEM((ROWS, D), BF16),
            pltpu.VMEM((ROWS, D), BF16),
            pltpu.VMEM((2, ROWS, 1), F32),
            pltpu.SemaphoreType.DMA((4,)),
            pltpu.SemaphoreType.DMA((2, 14 * C + 10)),
            pltpu.SemaphoreType.REGULAR,
        ],
        compiler_params=pltpu.CompilerParams(
            collective_id=0, has_side_effects=True, vmem_limit_bytes=40 * 1024 * 1024
        ),
        cost_estimate=pl.CostEstimate(
            flops=2_600_000_000, bytes_accessed=2_000_000, transcendentals=500_000
        ),
        name="pairs",
    )(
        log_temp.reshape(1, 1),
        bias.reshape(1, 1),
        pltpu.with_memory_space_constraint(images, pltpu.HBM),
        pltpu.with_memory_space_constraint(texts, pltpu.HBM),
    )
    return pl.pallas_call(
        store,
        out_shape=(out, out),
        in_specs=[vmem, vmem],
        out_specs=(hbm, hbm),
        scratch_shapes=[pltpu.SemaphoreType.DMA((2,))],
        compiler_params=pltpu.CompilerParams(vmem_limit_bytes=2 * 1024 * 1024),
        name="store",
    )(*sums)


def solution(mesh):
    return jax.shard_map(
        per_device,
        mesh=mesh,
        in_specs=(P(("grp", "blk"), None), P(("grp", "blk"), None), P(), P()),
        out_specs=(P(("grp", "blk"), None), P(("grp", "blk"), None)),
        check_vma=False,
    )
```

time: 70 us -> 60 us (0.86)
  the two profiles are of different devices: /device:TPU:4 before, /device:TPU:192 now
where the time goes in v2:
time: 60 us; the launch traced here: 59.9 us
  Pallas kernels  57.9 us (96%)
  between operations  1.93 us (3%)
    pallas_call x1, Pallas kernels, per_device(): pl.pallas_call(kernel, out_shape=(out, out), in_specs=[vmem] * 2 + [hbm]...  56.9 us

profile of v2, /device:TPU:192, one launch (start us, length us, event | category | flops | bytes accessed | tf_op | source)
XLA Modules:
  0.0 59.9 jit_solution(8696657383973311801)
XLA Ops:
  1.9 56.9 %pairs.1 = (f32[128,1152]{1,0:T(8,128)S(1)}, f32[128,1152]{1,0:T(8,128)S(1)}) custom-call(f32[1,1]{1,0:T(1,128)} %bitcast.2.temp_ref, f32[1,1]{1,0:T(1,128)} %bitcast.3.bias_ref, bf16[128,1152]{1,0:T(8,128)(2,1)} %img_ref.1, bf16[128,1152]{1,0:T(8,128)(2,1)} %txt_ref.1), custom_call_target="tpu_custom_call" | custom-call | flops 2600000000 | bytes 2000000 | tf_op jit(solution)/shard_map/pairs/pallas_call | solution.py:343
  58.8 1.0 %store.1 = (f32[128,1152]{1,0:T(8,128)}, f32[128,1152]{1,0:T(8,128)}) custom-call(f32[128,1152]{1,0:T(8,128)S(1)} %get-tuple-element.4.gi_ref, f32[128,1152]{1,0:T(8,128)S(1)} %get-tuple-element.5.gt_ref), custom_call_target="tpu_custom_call" | custom-call | tf_op jit(solution)/shard_map/store/pallas_call | solution.py:387

commit v3 on v2

--- a/solution.py
+++ b/solution.py
@@ -8,6 +8,7 @@
 MESH = pl.DeviceIdType.MESH
 ROWS = 128
 D = 1152
+RING = 8
 C = 4
 H = C // 2
 R = ROWS // C
@@ -41,8 +42,12 @@
     return (upstream - unit * inner) * rcp
 
 
-def rank(b):
+def rank_block(b):
     return jnp.where((b // 2) % 8 == 0, 0, 1000) + (b % 2) * 100 + b
+
+
+def rank_ring(y):
+    return jnp.where(y < RING // 2, y, RING + 3 - y)
 
 
 def chunk(c):
@@ -90,7 +95,11 @@
     mate = (g + 1 - 2 * (g % 2), b)
     near_blk = [(b + n_blk + o) % n_blk for o in OFFSETS]
     near = [(g, n) for n in near_blk]
-    earlier = [rank(n) < rank(b) for n in near_blk]
+    y_rank = rank_ring(g // 2)
+    fore_known = rank_ring(fore[0] // 2) < y_rank
+    back_known = rank_ring(back[0] // 2) < y_rank
+    mate_known = g % 2 == 1
+    earlier = [rank_block(n) < rank_block(b) for n in near_blk]
 
     loads = []
     for i, (src, dst) in enumerate(((txt_ref, txt_v), (img_ref, img_v))):
@@ -98,18 +107,27 @@
         load.start()
         loads.append(load)
 
+    partners = [(fore, fore_known, 1), (back, back_known, 0), (mate, mate_known, 2)]
+    partners += [(dev, known, 3) for dev, known in zip(near, earlier)]
     barrier = pltpu.get_barrier_semaphore()
-    for dev in (fore, back, mate):
-        pl.semaphore_signal(barrier, inc=1, device_id=dev, device_id_type=MESH)
-    greeted = 3
-    for dev, known in zip(near, earlier):
+    greeted = 0
+    for dev, known, _ in partners:
 
         @pl.when(jnp.logical_not(known))
         def _():
             pl.semaphore_signal(barrier, inc=1, device_id=dev, device_id_type=MESH)
 
         greeted = greeted + known.astype(jnp.int32)
-    pl.semaphore_wait(barrier, greeted)
+
+    @pl.when(greeted > 0)
+    def _():
+        pl.semaphore_wait(barrier, greeted)
+
+    for dev, known, place in partners:
+
+        @pl.when(known)
+        def _():
+            pl.semaphore_signal(ready.at[place], inc=1, device_id=dev, device_id_type=MESH)
 
     pending = []
     count = [0]
@@ -139,15 +157,29 @@
     gather_f = {}
     gather_b = {}
     for c in range(C):
-        d = C - 1 - c
-        gather_f[1, c] = send(txt_ref.at[chunk(c)], ring.at[0, chunk(c)], fore)
-        gather_b[1, d] = send(txt_ref.at[chunk(d)], ring.at[0, upper(d)], back)
-    mate_copy = send(img_ref, mate_raw, mate)
-    for dev, known in zip(near, earlier):
+        gather_f[1, c] = prepare(txt_ref.at[chunk(c)], ring.at[0, chunk(c)], fore)
+    for c in reversed(range(C)):
+        gather_b[1, c] = prepare(txt_ref.at[chunk(c)], ring.at[0, upper(c)], back)
+    mate_copy = prepare(img_ref, mate_raw, mate)
+    first = [
+        (list(gather_f[1, c] for c in range(C)), fore_known, 0),
+        (list(gather_b[1, c] for c in reversed(range(C))), back_known, 1),
+        ([mate_copy], mate_known, 2),
+    ]
+    for copies, known, _ in first:
 
         @pl.when(known)
         def _():
-            pl.semaphore_signal(ready, inc=1, device_id=dev, device_id_type=MESH)
+            for copy in copies:
+                copy.start()
+
+    for copies, known, place in first:
+
+        @pl.when(jnp.logical_not(known))
+        def _():
+            pl.semaphore_wait(ready.at[place], 1)
+            for copy in copies:
+                copy.start()
 
     for load in loads:
         load.wait()
@@ -221,9 +253,18 @@
     for c in range(H, C):
         forward(2, c)
     own_step()
-    forward(3, 0)
+    for c in range(H // 2):
+        forward(3, c)
     ring_step(1)
-    forward(3, 1)
+    answers = len(near) - sum(known.astype(jnp.int32) for known in earlier)
+
+    @pl.when(answers > 0)
+    def _():
+        pl.semaphore_wait(ready.at[3], answers)
+
+    send_near([jnp.logical_not(known) for known in earlier])
+    for c in range(H // 2, H):
+        forward(3, c)
     ring_step(2)
     for c in range(H, C):
         forward(3, c)
@@ -244,14 +285,6 @@
         d = C - 1 - c
         give_l(3, c, part[2, chunk(c)])
         give_r(3, d, part[2, upper(d)])
-
-    answers = 3 + len(near) - greeted
-
-    @pl.when(answers > 0)
-    def _():
-        pl.semaphore_wait(ready, answers)
-
-    send_near([jnp.logical_not(known) for known in earlier])
 
     for c in range(H):
         gather_f[4, c].wait_recv()
@@ -284,14 +317,14 @@
     for c in range(H):
         relay(2, c)
 
+    for c in range(H):
+        relay(1, c)
+
     for copy in near_copies:
         copy.wait_recv()
     texts = near_txt[...]
     coef = negative(score(imgs[0:ROWS], texts))
     img_acc[0:ROWS] += dot_nn(coef, texts)
-
-    for c in range(H):
-        relay(1, c)
 
     others = near_img[...]
     coef = negative(score(own_txt[...], others))
@@ -369,7 +402,7 @@
             pltpu.VMEM((2, ROWS, 1), F32),
             pltpu.SemaphoreType.DMA((4,)),
             pltpu.SemaphoreType.DMA((2, 14 * C + 10)),
-            pltpu.SemaphoreType.REGULAR,
+            pltpu.SemaphoreType.REGULAR((4,)),
         ],
         compiler_params=pltpu.CompilerParams(
             collective_id=0, has_side_effects=True, vmem_limit_bytes=40 * 1024 * 1024

time: 60 us -> 59.1 us (0.985)
  the two profiles are of different devices: /device:TPU:192 before, /device:TPU:150 now
where the time goes in v3:
time: 59.1 us; the launch traced here: 59 us
  Pallas kernels  57.1 us (97%)
  between operations  1.93 us (3%)
    pallas_call x1, Pallas kernels, per_device(): pl.pallas_call(kernel, out_shape=(out, out), in_specs=[vmem] * 2 + [hbm]...  56 us

profile of v3, /device:TPU:150, one launch (start us, length us, event | category | flops | bytes accessed | tf_op | source)
XLA Modules:
  0.0 59.0 jit_solution(7809968170853326870)
XLA Ops:
  1.9 56.0 %pairs.1 = (f32[128,1152]{1,0:T(8,128)S(1)}, f32[128,1152]{1,0:T(8,128)S(1)}) custom-call(f32[1,1]{1,0:T(1,128)} %bitcast.2.temp_ref, f32[1,1]{1,0:T(1,128)} %bitcast.3.bias_ref, bf16[128,1152]{1,0:T(8,128)(2,1)} %img_ref.1, bf16[128,1152]{1,0:T(8,128)(2,1)} %txt_ref.1), custom_call_target="tpu_custom_call" | custom-call | flops 2600000000 | bytes 2000000 | tf_op jit(solution)/shard_map/pairs/pallas_call | solution.py:376
  58.0 1.0 %store.1 = (f32[128,1152]{1,0:T(8,128)}, f32[128,1152]{1,0:T(8,128)}) custom-call(f32[128,1152]{1,0:T(8,128)S(1)} %get-tuple-element.4.gi_ref, f32[128,1152]{1,0:T(8,128)S(1)} %get-tuple-element.5.gt_ref), custom_call_target="tpu_custom_call" | custom-call | tf_op jit(solution)/shard_map/store/pallas_call | solution.py:420

commit v4 on v3

--- a/solution.py
+++ b/solution.py
@@ -308,17 +308,21 @@
         sums_r[k, d].wait_recv()
         give_r(k, d, part[k - 1, upper(d)] + in_r[k, chunk(d)].astype(F32))
 
+    for c in range(H):
+        relay(3, c)
     for c in range(H, C):
         relay(2, c)
     for c in range(H):
-        relay(3, c)
+        relay(2, c)
     for c in range(H, C):
         relay(1, c)
-    for c in range(H):
-        relay(2, c)
 
     for c in range(H):
         relay(1, c)
+
+    recent = 4 * H
+    for copy in pending[:-recent]:
+        copy.wait_send()
 
     for copy in near_copies:
         copy.wait_recv()
@@ -354,7 +358,7 @@
             norms[1, chunk(d)],
             txt_acc[chunk(d)] + in_r[0, chunk(d)].astype(F32),
         )
-    for copy in pending:
+    for copy in pending[-recent:]:
         copy.wait_send()
 
 

time: 59.1 us -> 59 us (level)
  no operation moved by 1% of the time
where the time goes in v4:
time: 59 us; the launch traced here: 58.9 us
  Pallas kernels  57 us (97%)
  between operations  1.93 us (3%)
    pallas_call x1, Pallas kernels, per_device(): pl.pallas_call(kernel, out_shape=(out, out), in_specs=[vmem] * 2 + [hbm]...  55.9 us

profile of v4, /device:TPU:150, one launch (start us, length us, event | category | flops | bytes accessed | tf_op | source)
XLA Modules:
  0.0 58.9 jit_solution(1548754230479963405)
XLA Ops:
  1.9 55.9 %pairs.1 = (f32[128,1152]{1,0:T(8,128)S(1)}, f32[128,1152]{1,0:T(8,128)S(1)}) custom-call(f32[1,1]{1,0:T(1,128)} %bitcast.2.temp_ref, f32[1,1]{1,0:T(1,128)} %bitcast.3.bias_ref, bf16[128,1152]{1,0:T(8,128)(2,1)} %img_ref.1, bf16[128,1152]{1,0:T(8,128)(2,1)} %txt_ref.1), custom_call_target="tpu_custom_call" | custom-call | flops 2600000000 | bytes 2000000 | tf_op jit(solution)/shard_map/pairs/pallas_call | solution.py:380
  57.9 1.0 %store.1 = (f32[128,1152]{1,0:T(8,128)}, f32[128,1152]{1,0:T(8,128)}) custom-call(f32[128,1152]{1,0:T(8,128)S(1)} %get-tuple-element.4.gi_ref, f32[128,1152]{1,0:T(8,128)S(1)} %get-tuple-element.5.gt_ref), custom_call_target="tpu_custom_call" | custom-call | tf_op jit(solution)/shard_map/store/pallas_call | solution.py:424

commit v5 on v4

--- a/solution.py
+++ b/solution.py
@@ -247,11 +247,11 @@
         forward(1, c)
     for c in range(H):
         forward(2, c)
+    send_near(earlier)
+    for c in range(H, C):
+        forward(2, c)
     mate_copy.wait_recv()
-    send_near(earlier)
     imgs[ROWS : 2 * ROWS] = unit_half(mate_raw[...])
-    for c in range(H, C):
-        forward(2, c)
     own_step()
     for c in range(H // 2):
         forward(3, c)

time: 59 us -> 59 us (level)
  no operation moved by 1% of the time
where the time goes in v5:
time: 59 us; the launch traced here: 58.9 us
  Pallas kernels  57 us (97%)
  between operations  1.93 us (3%)
    pallas_call x1, Pallas kernels, per_device(): pl.pallas_call(kernel, out_shape=(out, out), in_specs=[vmem] * 2 + [hbm]...  55.9 us

profile of v5, /device:TPU:150, one launch (start us, length us, event | category | flops | bytes accessed | tf_op | source)
XLA Modules:
  0.0 58.9 jit_solution(8318407796106745252)
XLA Ops:
  1.9 55.9 %pairs.1 = (f32[128,1152]{1,0:T(8,128)S(1)}, f32[128,1152]{1,0:T(8,128)S(1)}) custom-call(f32[1,1]{1,0:T(1,128)} %bitcast.2.temp_ref, f32[1,1]{1,0:T(1,128)} %bitcast.3.bias_ref, bf16[128,1152]{1,0:T(8,128)(2,1)} %img_ref.1, bf16[128,1152]{1,0:T(8,128)(2,1)} %txt_ref.1), custom_call_target="tpu_custom_call" | custom-call | flops 2600000000 | bytes 2000000 | tf_op jit(solution)/shard_map/pairs/pallas_call | solution.py:380
  57.9 1.0 %store.1 = (f32[128,1152]{1,0:T(8,128)}, f32[128,1152]{1,0:T(8,128)}) custom-call(f32[128,1152]{1,0:T(8,128)S(1)} %get-tuple-element.4.gi_ref, f32[128,1152]{1,0:T(8,128)S(1)} %get-tuple-element.5.gt_ref), custom_call_target="tpu_custom_call" | custom-call | tf_op jit(solution)/shard_map/store/pallas_call | solution.py:424
